TPU v7x, 512 devices: a whole 4x8x8 slice. The times are simulated.
512 devices in a mesh: row: 32 (over y_lo, x, core), col: 16 (over y_hi, z).
Axes of the slice: x: 4, y: 8 (y_hi: 2, y_lo: 4; y = y_hi * 4 + y_lo), z: 8, core: 2. Of those that a mesh axis runs over, the one named last changes fastest.
Arguments:
- queries: bfloat16 [16384, 2048], P('row', 'col'), may hold values from -8 to 8
- keys: bfloat16 [16384, 512], P('row'), may hold values from -8 to 8
- values: bfloat16 [16384, 512], P('row'), may hold values from -6 to 6
- out_weight: bfloat16 [2048, 4096], P('col'), may hold values from -0.75 to 0.75
- slot_span: int32 [32], replicated, may hold values from 0 to 31, each once
Outputs:
- mixed: bfloat16 [16384, 4096], P('row', 'col')
Inputs may be any that keep to these rules, and one draw needn't show every extreme that they name: `slot_span`: each of the 32 sequence blocks is stored in exactly one slot.
All inputs are finite; a program needn't handle non-finite values.
Results may differ from a plain program's by a relative error of at most 0.03.
Values may be sent and summed in bfloat16 or wider, within the bound.
A program may use at most 64 MiB of HBM per device.

v0:
```python
import math

import jax
import jax.numpy as jnp
from jax import lax
from jax.sharding import PartitionSpec as P

HEAD_SIZE = 128
GROUP = 4


NEG = -1e30


def tile_scores(query_block, query_pos, key_block, value_block, key_pos):
    visible = key_pos[None, :] <= query_pos[:, None]
    scale = query_block.shape[-1] ** (-0.5)
    scores = (
        jnp.einsum("qkgd,skd->kgqs", query_block, key_block, preferred_element_type=jnp.float32)
        * scale
    )
    scores = jnp.where(visible[None, None], scores, jnp.float32(NEG))
    peak = jnp.max(scores, axis=-1)
    weights = jnp.where(
        visible[None, None], jnp.exp(scores - peak[..., None]), jnp.float32(0.0)
    ).astype(jnp.bfloat16)
    total = jnp.sum(weights, axis=-1, dtype=jnp.float32)
    summed = jnp.einsum("kgqs,skd->qkgd", weights, value_block, preferred_element_type=jnp.float32)
    return (summed, jnp.transpose(peak, (2, 0, 1)), jnp.transpose(total, (2, 0, 1)))


def tile_checked(query_block, query_pos, key_block, value_block, key_pos):
    return tile_scores(query_block, query_pos, key_block, value_block, key_pos)


def combine(state, fresh):
    top = jnp.maximum(state[1], fresh[1])
    keep_old = jnp.exp(state[1] - top)
    keep_new = jnp.exp(fresh[1] - top)
    return (
        state[0] * keep_old[..., None] + fresh[0] * keep_new[..., None],
        top,
        state[2] * keep_old + fresh[2] * keep_new,
    )


def local(queries, keys, values, out_weight, slot_span):
    tok = queries.shape[0]
    row_index = lax.axis_index("row")
    col_index = lax.axis_index("col")
    heads = queries.shape[1] // HEAD_SIZE
    kv_local = max(1, heads // GROUP)
    per_kv = heads // kv_local
    first = col_index * heads // GROUP
    key_mine = lax.dynamic_slice_in_dim(keys, first * HEAD_SIZE, kv_local * HEAD_SIZE, 1)
    value_mine = lax.dynamic_slice_in_dim(values, first * HEAD_SIZE, kv_local * HEAD_SIZE, 1)
    offsets = jnp.arange(tok, dtype=jnp.int32)
    all_pos = (slot_span[:, None] * tok + offsets[None, :]).reshape(-1)
    my_pos = lax.dynamic_slice_in_dim(all_pos, row_index * tok, tok, 0)
    query_local = queries.reshape(tok, kv_local, per_kv, HEAD_SIZE)
    start_state = (
        jnp.zeros((tok, kv_local, per_kv, HEAD_SIZE), jnp.float32),
        jnp.full((tok, kv_local, per_kv), NEG, jnp.float32),
        jnp.zeros((tok, kv_local, per_kv), jnp.float32),
    )
    piece = (
        lax.all_gather(key_mine, "row", axis=0, tiled=True),
        lax.all_gather(value_mine, "row", axis=0, tiled=True),
    )
    count = piece[0].shape[0]
    block = math.gcd(count, 2048)
    steps = count // block
    key_steps = piece[0].reshape(steps, block, kv_local, HEAD_SIZE)
    value_steps = piece[1].reshape(steps, block, kv_local, HEAD_SIZE)
    pos_steps = all_pos.reshape(steps, block)

    def one_step(state, items):
        fresh = tile_checked(query_local, my_pos, items[0], items[1], items[2])
        return (combine(state, fresh), None)

    final, unused = lax.scan(one_step, start_state, (key_steps, value_steps, pos_steps))
    whole_sum, unused_peak, whole_total = final
    attended = (
        (whole_sum / whole_total[..., None]).astype(jnp.bfloat16).reshape(tok, heads * HEAD_SIZE)
    )
    term = jnp.dot(attended, out_weight, preferred_element_type=jnp.float32)
    return lax.psum_scatter(term.astype(jnp.bfloat16), "col", scatter_dimension=1, tiled=True)


def solution(mesh):
    in_specs = (P("row", "col"), P("row", None), P("row", None), P("col", None), P())
    out_specs = P("row", "col")
    return jax.shard_map(local, mesh=mesh, in_specs=in_specs, out_specs=out_specs, check_vma=False)
```

profile of v0, /device:TPU:10, one launch (start us, length us, event | category | flops | bytes accessed | tf_op | source)
XLA Modules:
  0.0 463.9 jit_solution(12669345625112214281)
XLA Ops:
  6.5 1.7 constant_dynamic-slice_fusion.2
  8.3 1.6 constant_dynamic-slice_fusion.1
  11.0 67.7 %all-gather.3.cloned.1.call-done = bf16[16384,128]{1,0:T(8,128)(2,1)} async-done(((bf16[512,128]{1,0:T(8,128)(2,1)}), bf16[16384,128]{1,0:T(8,128)(2,1)}) %all-gather.3.cloned.1.call-update) | async-done | bytes 4194320 | tf_op jit(solution)/shard_map/all_gather | solution.py:67
  78.7 66.7 %all-gather.5.cloned.1.call-done = bf16[16384,128]{1,0:T(8,128)(2,1)} async-done(((bf16[512,128]{1,0:T(8,128)(2,1)}), bf16[16384,128]{1,0:T(8,128)(2,1)}) %all-gather.5.cloned.1.call-update) | async-done | bytes 4194320 | tf_op jit(solution)/shard_map/all_gather | solution.py:68
  145.5 72.1 %while.15 = (s32[]{:T(128)}, f32[512,1,1,128]{0,3,2,1:T(8,128)S(1)}, f32[512,1,1]{0,2,1:T(1,128)S(1)}, f32[512,1,1]{0,2,1:T(1,128)S(1)}, s32[8,2048]{1,0:T(8,128...) while((s32[]{:T(128)}, ...), condition=%wide.region_3.4_spmd.clone, body=%wide.region_0.3_spmd.clone.sunk | while | flops 556010496 | bytes 31141016 | solution.py:81
  145.5 1.9 fusion.38
  147.4 1.9 copy-done.1
  149.4 1.2 convert_reduce_fusion.2
  150.7 3.8 fusion.40
  154.5 1.9 fusion.38
  156.4 1.9 copy-done.1
  159.7 3.8 fusion.40
  163.5 1.9 fusion.38
  165.5 1.9 copy-done.1
  168.7 3.8 fusion.40
  172.5 1.9 fusion.38
  174.5 1.9 copy-done.1
  177.7 3.8 fusion.40
  181.6 1.9 fusion.38
  183.5 1.9 copy-done.1
  186.7 3.8 fusion.40
  190.6 1.9 fusion.38
  192.5 1.9 copy-done.1
  195.8 3.8 fusion.40
  199.6 1.9 fusion.38
  201.5 1.9 copy-done.1
  204.8 3.8 fusion.40
  208.6 1.9 fusion.38
  210.6 1.9 copy-done.1
  213.8 3.8 fusion.40
  217.6 3.2 convolution_convert_fusion
  220.9 236.5 %reduce-scatter.2.cloned.1.call-done = bf16[512,256]{1,0:T(8,128)(2,1)} async-done(((bf16[512,4096]{1,0:T(8,128)(2,1)}), bf16[512,256]{1,0:T(8,128)(2,1)}) %reduce-scatter.2.cloned.1.call-update) | async-done | bytes 262160 | tf_op jit(solution)/shard_map/reduce_scatter | solution.py:87
  (52 shorter events, 10.3 us)
Async XLA Ops:
  6.5 211.1 %copy-start = (bf16[128,4096]{1,0:T(8,128)(2,1)S(1)}, bf16[128,4096]{1,0:T(8,128)(2,1)}, u32[]{:S(2)}) copy-start(bf16[128,4096]{1,0:T(8,128)(2,1)} %param.10) | copy-start | bytes 3145732
  6.5 72.2 %all-gather.3.cloned.1.call-start = ((), (), s32[]{:S(2)}) async-start(), calls=%async_computation.1 | async-start | bytes 4325376 | tf_op jit(solution)/shard_map/all_gather | solution.py:67
  8.2 137.2 %all-gather.5.cloned.1.call-start = ((), (), s32[]{:S(2)}) async-start(), calls=%async_computation.2 | async-start | bytes 4325376 | tf_op jit(solution)/shard_map/all_gather | solution.py:68
  9.9 447.5 %reduce-scatter.2.cloned.1.call-start = ((), (), s32[]{:S(2)}) async-start(), calls=%async_computation.3 | async-start | bytes 4456448 | tf_op jit(solution)/shard_map/reduce_scatter | solution.py:87
  147.4 2.0 copy-start.1
  156.4 2.0 copy-start.1
  165.5 2.0 copy-start.1
  174.5 2.0 copy-start.1
  183.5 2.0 copy-start.1
  192.5 2.0 copy-start.1
  201.5 2.0 copy-start.1
  210.6 2.0 copy-start.1
Sparse Core Ops, SparseCore 0:
  9.5 69.1 all-gather.2
  80.9 64.5 all-gather.4
  221.0 236.3 reduce-scatter.1
where the time goes:
time: 464 us
  waiting for transfers between devices  371 us (80%)
  matrix products  49 us (11%)
  local copies, waits for them, and re-layouts  19.2 us (4%)
  between operations  13.2 us (3%)
  other arithmetic  11 us (2%)
    reduce_scatter x1, waiting for transfers between devices, local(): lax.psum_scatter(term.astype(jnp.bfloat16), 'col', scatter_dimension=1, t...  236 us
    all_gather x1, waiting for transfers between devices, local(): lax.all_gather(key_mine, 'row', axis=0, tiled=True)  67.7 us
    all_gather x1, waiting for transfers between devices, local(): lax.all_gather(value_mine, 'row', axis=0, tiled=True)  66.7 us
    dot_general x8, matrix products, tile_scores(): jnp.einsum('kgqs,skd->qkgd', weights, value_block, preferred_element_type...  30.3 us
    while x16, local copies, waits for them, and re-layouts  15.6 us
    dot_general x8, matrix products, tile_scores(): jnp.einsum('qkgd,skd->kgqs', query_block, key_block, preferred_element_ty...  15.5 us
    reduce_sum x8, other arithmetic, tile_scores(): total = jnp.sum(weights, axis=-1, dtype=jnp.float32)  10 us
  transfers between devices with their start and end apart: 3, of which 3 were waited for; matrix products, arithmetic and copies ran while one was open for 1% of the time, Pallas kernels for 0%

commit v1 on v0

v1 whole, which is shorter than its diff:
```python
import math

import jax
import jax.numpy as jnp
from jax import lax
from jax.experimental import pallas as pl
from jax.experimental.pallas import tpu as pltpu
from jax.sharding import PartitionSpec as P

MESH = pl.DeviceIdType.MESH
TOK = 512
HALF = TOK // 2
HEAD = 128
NX, NY, NZ = 4, 8, 8
OUT = 256
ROWS = 128
NB = TOK // ROWS
FLOOR = -1e30
HIDDEN = 3e30
SCALE = HEAD**-0.5 * math.log2(math.e)

FIRST = ((0, 0), (1, 0))
GROUPS = (
    ((0, 3), (0, 1), (3, 0)),
    ((1, 3), (1, 1), (2, 0), (0, 2)),
    ((3, 3), (3, 1), (1, 2)),
    ((2, 3), (2, 1), (3, 2)),
    ((2, 2),),
)
COPIES = 128


def kernel(
    span, queries, keys, values, weight, out,
    qbuf, kbuf, vbuf, wbuf, acc, peak, around, give, got, give_stat, got_stat, own_part, swap, swapped,
    send_sem, recv_sem, local_sem,
):
    row, col = lax.axis_index("row"), lax.axis_index("col")
    core, x, ylo = row % 2, (row // 2) % NX, row // (2 * NX)
    z, yhi = col % NZ, col // NZ
    y = yhi * 4 + ylo
    parity = y % 2
    toward = 1 - 2 * parity

    def device(xx, yy, zz, cc):
        xx, yy, zz = (xx + NX) % NX, (yy + NY) % NY, (zz + NZ) % NZ
        return (((yy % 4) * NX + xx) * 2 + cc, (yy // 4) * NZ + zz)

    def slot_row(yx, dx, dc):
        yy = (ylo // 2 + yx // 2) % 2 * 2 + (ylo + yx) % 2
        return (yy * NX + (x + dx) % NX) * 2 + (core + dc) % 2

    def at_y(dy):
        return device(x, y + dy, z, core)

    def at_x(dx):
        return device(x + dx, y, z, core)

    def at_z(dz):
        return device(x, y, z + dz, core)

    sibling = device(x, y, z, (core + 1) % 2)
    opposite = device(x, y + 4, z, core)

    barrier = pltpu.get_barrier_semaphore()
    peers = [at_y(toward), at_y(-toward), at_y(2), at_y(-2), opposite, at_x(1), at_x(-1), sibling]
    peers += [at_z(d) for d in range(1, NZ)]
    for peer in peers:
        pl.semaphore_signal(barrier, inc=1, device_id=peer, device_id_type=MESH)

    vbuf[:, :, :, :, HEAD:] = jnp.ones((4, NX, 2, HALF, HEAD), jnp.bfloat16)

    def tokens(ref, yy):
        yy = (yy + NY) % NY
        group = (yy // 4) * 2 + z // 4
        start = pl.multiple_of((yy % 2) * HALF, HALF)
        return ref.at[pl.ds(start, HALF), pl.ds(pl.multiple_of(group * HEAD, HEAD), HEAD)]

    def kslot(yx, dx, dc=0):
        return kbuf.at[yx, dx, dc]

    def vslot(yx, dx, dc=0):
        return vbuf.at[yx, dx, dc, :, pl.ds(0, HEAD)]

    own_weight = pl.ds(pl.multiple_of(col * OUT, OUT), OUT)
    other_weight = pl.ds(pl.multiple_of((1 - yhi) * (NZ * OUT) + z * OUT, OUT), OUT)
    here = [
        pltpu.make_async_copy(tokens(keys, y), kslot(0, 0), local_sem.at[0]),
        pltpu.make_async_copy(tokens(values, y), vslot(0, 0), local_sem.at[1]),
        pltpu.make_async_copy(queries, qbuf.at[pl.ds(0, TOK)], local_sem.at[2]),
        pltpu.make_async_copy(weight.at[:, own_weight], wbuf.at[pl.ds(0, HEAD), pl.ds(0, OUT)], local_sem.at[3]),
        pltpu.make_async_copy(weight.at[:, other_weight], wbuf.at[pl.ds(0, HEAD), pl.ds(OUT, OUT)], local_sem.at[4]),
    ]
    for copy in here:
        copy.start()
    pl.semaphore_wait(barrier, len(peers))

    started = []

    def push(src, dst, to):
        k = len(started)
        copy = pltpu.make_async_remote_copy(
            src_ref=src, dst_ref=dst, send_sem=send_sem.at[k], recv_sem=recv_sem.at[k], device_id=to, device_id_type=MESH
        )
        copy.start()
        started.append(copy)
        return copy

    arriving = {}

    def push_k(src, yx, dx, dc, to):
        arriving[yx, dx, dc, 0] = push(src, kslot(yx, dx, dc), to)

    def push_v(src, yx, dx, dc, to):
        arriving[yx, dx, dc, 1] = push(src, vslot(yx, dx, dc), to)

    def landed(yx, dx, dc):
        arriving[yx, dx, dc, 0].wait_recv()
        arriving[yx, dx, dc, 1].wait_recv()

    def across(yx, dx):
        push_k(kslot(yx, dx), yx, dx, 1, sibling)
        push_v(vslot(yx, dx), yx, dx, 1, sibling)

    def along_x(yx, k, v):
        push_k(k, yx, 3, 0, at_x(1))
        push_k(k, yx, 1, 0, at_x(-1))
        push_v(v, yx, 3, 0, at_x(1))
        push_v(v, yx, 1, 0, at_x(-1))

    def from_y(yx):
        landed(yx, 0, 0)
        along_x(yx, kslot(yx, 0), vslot(yx, 0))
        across(yx, 0)

    def from_x(yx):
        landed(yx, 3, 0)
        push_k(kslot(yx, 3), yx, 2, 0, at_x(1))
        across(yx, 3)
        landed(yx, 1, 0)
        push_v(vslot(yx, 1), yx, 2, 0, at_x(-1))
        across(yx, 1)

    def from_far(yx):
        landed(yx, 2, 0)
        across(yx, 2)

    def both(yx, dx):
        landed(yx, dx, 1)

    ask = push(queries, qbuf.at[pl.ds(TOK, TOK)], at_y(toward))
    push_k(tokens(keys, y + toward), 1, 0, 0, at_y(toward))
    push_k(tokens(keys, y - toward), 3, 0, 0, at_y(-toward))
    push_v(tokens(values, y + toward), 1, 0, 0, at_y(toward))
    push_v(tokens(values, y - toward), 3, 0, 0, at_y(-toward))
    along_x(0, tokens(keys, y), tokens(values, y))
    push_k(tokens(keys, y), 0, 0, 1, sibling)
    push_v(tokens(values, y), 0, 0, 1, sibling)
    push_k(tokens(keys, y + 2), 2, 0, 0, at_y(2))
    push_v(tokens(values, y - 2), 2, 0, 0, at_y(-2))
    half_rows = pl.multiple_of(core * (HEAD // 2), HEAD // 2)
    weights = []
    for d in range(1, NZ):
        zz = (z + d) % NZ
        for part, hi in ((0, yhi), (1, 1 - yhi)):
            columns = pl.ds(pl.multiple_of((hi * NZ + zz) * OUT, OUT), OUT)
            weights.append(
                push(
                    weight.at[pl.ds(half_rows, HEAD // 2), columns],
                    wbuf.at[pl.ds(d * HEAD + half_rows, HEAD // 2), pl.ds(part * OUT, OUT)],
                    at_z(d),
                )
            )
    for copy in here:
        copy.wait()

    my_span = (span[row], span[slot_row(1, 0, 0)])

    def hide(side, yx, dx, dc):
        return jnp.where(span[slot_row(yx, dx, dc)] < my_span[side], 0.0, HIDDEN).astype(jnp.float32)

    def step(group, side, block, first=False):
        at = pl.ds(side * TOK + block * ROWS, ROWS)
        query = qbuf[at, :]
        parts, top = [], None
        for yx, dx in group:
            k = kbuf[yx, dx].reshape(TOK, HEAD)
            scores = lax.dot_general(query, k, (((1,), (1,)), ((), ())), preferred_element_type=jnp.float32)
            for dc in range(2):
                part = scores[:, dc * HALF : (dc + 1) * HALF]
                seen = None
                if first and dc == 0 and (yx, side) in ((0, 0), (1, 1)):
                    i = lax.broadcasted_iota(jnp.int32, (ROWS, HALF), 0) + block * ROWS
                    j = lax.broadcasted_iota(jnp.int32, (ROWS, HALF), 1) + parity * HALF
                    seen = j <= i
                    hidden = None
                    shown = jnp.where(seen, part, jnp.float32(-HIDDEN))
                    part_top = jnp.maximum(shown[:, :HEAD], shown[:, HEAD:])
                else:
                    hidden = hide(side, yx, dx, dc)
                    part_top = jnp.maximum(part[:, :HEAD], part[:, HEAD:]) - hidden
                top = part_top if top is None else jnp.maximum(top, part_top)
                parts.append((part, hidden, seen))
        new = jnp.max(top, axis=1, keepdims=True) * SCALE
        if first:
            new = jnp.maximum(new, jnp.float32(FLOOR))
        else:
            old = peak[at, :]
            new = jnp.maximum(old, new)
            keep = jnp.exp2(old - new)[:, :1]
        new = jnp.broadcast_to(new, (ROWS, HEAD))
        total = None
        for n, (yx, dx) in enumerate(group):
            shares = []
            for part, hidden, seen in parts[2 * n : 2 * n + 2]:
                if seen is None:
                    power = part * SCALE - (new + hidden)[:, :1]
                else:
                    power = jnp.where(seen, part * SCALE - new[:, :1], jnp.float32(-HIDDEN))
                shares.append(jnp.exp2(power).astype(jnp.bfloat16))
            share = jnp.concatenate(shares, axis=1)
            value = vbuf[yx, dx].reshape(TOK, 2 * HEAD)
            term = jnp.dot(share, value, preferred_element_type=jnp.float32)
            total = term if total is None else total + term
        peak[at, :] = new
        acc[at, :] = total if first else acc[at, :] * keep + total

    def work(group, side, first=False):
        for block in range(NB):
            step(group, side, block, first)

    from_y(1)
    from_y(3)
    both(0, 0)
    ask.wait_recv()
    both(1, 0)
    work(FIRST, 0, True)
    from_x(0)
    work(FIRST, 1, True)
    from_y(2)
    for pair in GROUPS[0]:
        both(*pair)
    work(GROUPS[0], 0)
    from_x(1)
    work(GROUPS[0], 1)
    from_far(0)
    for pair in GROUPS[1]:
        both(*pair)
    work(GROUPS[1], 0)
    from_x(3)
    work(GROUPS[1], 1)
    from_far(1)
    for pair in GROUPS[2]:
        both(*pair)
    work(GROUPS[2], 0)
    from_x(2)
    work(GROUPS[2], 1)
    for copy in weights:
        copy.wait_recv()
    across_rows = [wbuf.at[pl.ds(d * HEAD + half_rows, HEAD // 2)] for d in range(1, NZ)]
    weights = [push(rows, rows, sibling) for rows in across_rows]
    from_far(3)
    for pair in GROUPS[3]:
        both(*pair)
    work(GROUPS[3], 0)
    from_far(2)
    work(GROUPS[3], 1)
    both(2, 2)

    given = []
    lane = lax.broadcasted_iota(jnp.int32, (ROWS, HEAD), 1)
    for block in range(NB):
        step(GROUPS[4], 1, block)
        at = pl.ds(TOK + block * ROWS, ROWS)
        here_rows = pl.ds(block * ROWS, ROWS)
        give[here_rows, :] = acc[at, :HEAD].astype(jnp.bfloat16)
        stat = jnp.where(lane == 0, peak[at, :], acc[at, HEAD:])
        give_stat[block] = stat.T[:8, :]
        given.append(
            (
                push(give.at[here_rows], got.at[here_rows], at_y(toward)),
                push(give_stat.at[block], got_stat.at[block], at_y(toward)),
            )
        )
    work(GROUPS[4], 0)

    rings = {}

    def cut(block, d):
        return around.at[pl.ds(block * ROWS, ROWS), pl.ds(d * HEAD, HEAD)]

    def send_z(block, d, to):
        src = (d - 1) if to == 1 else (d + 1) % NZ
        rings[block, d] = push(cut(block, src), cut(block, d), at_z(to))

    def combine(block):
        rows = pl.ds(block * ROWS, ROWS)
        for copy in given[block]:
            copy.wait_recv()
        stat = jnp.concatenate([got_stat[block], jnp.zeros((ROWS - 8, HEAD), jnp.float32)], axis=0).T
        peak_two, sum_two = stat[:, 0:1], stat[:, 1:2]
        peak_one, sum_one = peak[rows, :][:, :1], acc[rows, HEAD:][:, :1]
        top = jnp.maximum(peak_one, peak_two)
        one, two = jnp.exp2(peak_one - top), jnp.exp2(peak_two - top)
        total = acc[rows, :HEAD] * one + got[rows, :].astype(jnp.float32) * two
        around[rows, pl.ds(0, HEAD)] = (total / (sum_one * one + sum_two * two)).astype(jnp.bfloat16)
        send_z(block, 1, 1)
        send_z(block, NZ - 1, -1)

    def onward(block, stage):
        rings[block, stage].wait_recv()
        if stage < 3 or block % 2 == 0:
            send_z(block, stage + 1, 1)
        rings[block, NZ - stage].wait_recv()
        if stage < 3 or block % 2 == 1:
            send_z(block, NZ - stage - 1, -1)

    swaps = []

    def project(block):
        rings[block, 4].wait_recv()
        rows = pl.ds(block * ROWS, ROWS)
        part = jnp.dot(around[rows, :], wbuf[...], preferred_element_type=jnp.float32)
        own_part[rows, :] = part[:, :OUT]
        swap[rows, :] = part[:, OUT:].astype(jnp.bfloat16)
        swaps.append(push(swap.at[rows], swapped.at[rows], opposite))

    for turn in range(NB + 4):
        if turn < NB:
            combine(turn)
        if turn == 0:
            for copy in weights:
                copy.wait_recv()
        for stage in range(1, 5):
            block = turn - stage
            if 0 <= block < NB:
                if stage < 4:
                    onward(block, stage)
                else:
                    project(block)
    for block in range(NB):
        rows = pl.ds(block * ROWS, ROWS)
        swaps[block].wait_recv()
        out[rows, :] = (own_part[rows, :] + swapped[rows, :].astype(jnp.float32)).astype(jnp.bfloat16)
    for copy in started:
        copy.wait_send()


def local(queries, keys, values, out_weight, slot_span):
    vmem, anywhere = pl.BlockSpec(memory_space=pltpu.VMEM), pl.BlockSpec(memory_space=pl.ANY)
    return pl.pallas_call(
        kernel,
        out_shape=jax.ShapeDtypeStruct((TOK, OUT), jnp.bfloat16),
        in_specs=[pl.BlockSpec(memory_space=pltpu.SMEM), vmem, vmem, vmem, anywhere],
        out_specs=vmem,
        scratch_shapes=[
            pltpu.VMEM((2 * TOK, HEAD), jnp.bfloat16),
            pltpu.VMEM((4, NX, 2, HALF, HEAD), jnp.bfloat16),
            pltpu.VMEM((4, NX, 2, HALF, 2 * HEAD), jnp.bfloat16),
            pltpu.VMEM((NZ * HEAD, 2 * OUT), jnp.bfloat16),
            pltpu.VMEM((2 * TOK, 2 * HEAD), jnp.float32),
            pltpu.VMEM((2 * TOK, HEAD), jnp.float32),
            pltpu.VMEM((TOK, NZ * HEAD), jnp.bfloat16),
            pltpu.VMEM((TOK, HEAD), jnp.bfloat16),
            pltpu.VMEM((TOK, HEAD), jnp.bfloat16),
            pltpu.VMEM((NB, 8, ROWS), jnp.float32),
            pltpu.VMEM((NB, 8, ROWS), jnp.float32),
            pltpu.VMEM((TOK, OUT), jnp.float32),
            pltpu.VMEM((TOK, OUT), jnp.bfloat16),
            pltpu.VMEM((TOK, OUT), jnp.bfloat16),
            pltpu.SemaphoreType.DMA((COPIES,)),
            pltpu.SemaphoreType.DMA((COPIES,)),
            pltpu.SemaphoreType.DMA((5,)),
        ],
        compiler_params=pltpu.CompilerParams(
            collective_id=0, has_side_effects=True, vmem_limit_bytes=56 * 2**20
        ),
        cost_estimate=pl.CostEstimate(flops=9 * 10**9, bytes_accessed=3 * 10**6, transcendentals=9 * 10**6),
        name="attend_and_project",
    )(slot_span, queries, keys, values, out_weight)


def solution(mesh):
    in_specs = (P("row", "col"), P("row", None), P("row", None), P("col", None), P())
    return jax.shard_map(local, mesh=mesh, in_specs=in_specs, out_specs=P("row", "col"), check_vma=False)
```

time: 464 us -> 83 us (0.18)
  the two profiles are of different devices: /device:TPU:10 before, /device:TPU:72 now
where the time goes in v1:
time: 83 us; the launch traced here: 82.8 us
  Pallas kernels  81.1 us (98%)
  local copies, waits for them, and re-layouts  1.67 us (2%)
    pallas_call x1, Pallas kernels, local(): pl.pallas_call(kernel, out_shape=jax.ShapeDtypeStruct((TOK, OUT), jnp.bfl...  81.1 us
    unnamed x1, local copies, waits for them, and re-layouts  1.67 us

profile of v1, /device:TPU:72, one launch (start us, length us, event | category | flops | bytes accessed | tf_op | source)
XLA Modules:
  0.0 82.8 jit_solution(4066784087751227318)
XLA Ops:
  0.0 81.1 %attend_and_project.1 = bf16[512,256]{1,0:T(8,128)(2,1)} custom-call(s32[32]{0:T(128)} %span.1, bf16[512,128]{1,0:T(8,128)(2,1)} %queries.1, bf16[512,512]{1,0:T(8,128)(2,1)} %keys.1, bf16[512,512]{1,0:T(8,128)(2,1)} %values.1, bf16[128,4096]{1,0:T(8,128)(2,1)} %weight.1), custom_call_target="tpu_custom_call" | custom-call | flops 8999999488 | bytes 3000000 | tf_op jit(solution)/shard_map/attend_and_project/pallas_call | solution.py:351
  81.1 1.7 %copy.7 = bf16[512,256]{1,0:T(8,128)(2,1)} copy(bf16[512,256]{1,0:T(8,128)(2,1)} %attend_and_project.1) | data formatting | bytes 524288

commit v2 on v1

v2 whole, which is shorter than its diff:
```python
import math

import jax
import jax.numpy as jnp
from jax import lax
from jax.experimental import pallas as pl
from jax.experimental.pallas import tpu as pltpu
from jax.sharding import PartitionSpec as P

MESH = pl.DeviceIdType.MESH
TOK = 512
HALF = TOK // 2
HEAD = 128
NX, NY, NZ = 4, 8, 8
OUT = 256
ROWS = 256
STAT = 128
NB = TOK // ROWS
FLOOR = -1e30
HIDDEN = 3e30
SCALE = HEAD**-0.5 * math.log2(math.e)

LAST = ((2, 2),)
COPIES = 180
CUTS = 4
CUT = TOK // CUTS
LAG = 1
DIRECT = ()
TURNS = [(cut, stage) for stage in range(5) for cut in range(CUTS)]


def kernel(
    span, queries, keys, values, weight, out,
    qbuf, kbuf, vbuf, wbuf, acc, peak, around, give, got, give_stat, got_stat, own_part, swap, swapped,
    send_sem, recv_sem, local_sem,
):
    row, col = lax.axis_index("row"), lax.axis_index("col")
    core, x, ylo = row % 2, (row // 2) % NX, row // (2 * NX)
    z, yhi = col % NZ, col // NZ
    y = yhi * 4 + ylo
    parity = y % 2
    toward = 1 - 2 * parity

    def device(xx, yy, zz, cc):
        xx, yy, zz = (xx + NX) % NX, (yy + NY) % NY, (zz + NZ) % NZ
        return (((yy % 4) * NX + xx) * 2 + cc, (yy // 4) * NZ + zz)

    def slot_row(yx, dx, dc):
        yy = (ylo // 2 + yx // 2) % 2 * 2 + (ylo + yx) % 2
        return (yy * NX + (x + dx) % NX) * 2 + (core + dc) % 2

    def at_y(dy):
        return device(x, y + dy, z, core)

    def at_x(dx):
        return device(x + dx, y, z, core)

    def at_z(dz):
        return device(x, y, z + dz, core)

    sibling = device(x, y, z, (core + 1) % 2)
    opposite = device(x, y + 4, z, core)

    barrier = pltpu.get_barrier_semaphore()
    peers = [at_y(toward), at_y(-toward), at_y(2), at_y(-2), opposite, at_x(1), at_x(-1), at_x(2), sibling]
    peers += [at_z(d) for d in range(1, NZ)]
    for peer in peers:
        pl.semaphore_signal(barrier, inc=1, device_id=peer, device_id_type=MESH)

    vbuf[:, :, :, :, HEAD:] = jnp.ones((4, NX, 2, HALF, HEAD), jnp.bfloat16)

    def tokens(ref, yy):
        yy = (yy + NY) % NY
        group = (yy // 4) * 2 + z // 4
        start = pl.multiple_of((yy % 2) * HALF, HALF)
        return ref.at[pl.ds(start, HALF), pl.ds(pl.multiple_of(group * HEAD, HEAD), HEAD)]

    def kslot(yx, dx, dc=0):
        return kbuf.at[yx, dx, dc]

    def vslot(yx, dx, dc=0):
        return vbuf.at[yx, dx, dc, :, pl.ds(0, HEAD)]

    own_weight = pl.ds(pl.multiple_of(col * OUT, OUT), OUT)
    other_weight = pl.ds(pl.multiple_of((1 - yhi) * (NZ * OUT) + z * OUT, OUT), OUT)
    here = [
        pltpu.make_async_copy(tokens(keys, y), kslot(0, 0), local_sem.at[0]),
        pltpu.make_async_copy(tokens(values, y), vslot(0, 0), local_sem.at[1]),
        pltpu.make_async_copy(queries, qbuf.at[pl.ds(0, TOK)], local_sem.at[2]),
        pltpu.make_async_copy(weight.at[:, own_weight], wbuf.at[pl.ds(0, HEAD), pl.ds(0, OUT)], local_sem.at[3]),
        pltpu.make_async_copy(weight.at[:, other_weight], wbuf.at[pl.ds(0, HEAD), pl.ds(OUT, OUT)], local_sem.at[4]),
    ]
    for copy in here:
        copy.start()
    pl.semaphore_wait(barrier, len(peers))

    started = []

    def push(src, dst, to):
        k = len(started)
        copy = pltpu.make_async_remote_copy(
            src_ref=src, dst_ref=dst, send_sem=send_sem.at[k], recv_sem=recv_sem.at[k], device_id=to, device_id_type=MESH
        )
        copy.start()
        started.append(copy)
        return copy

    arriving = {}

    def push_k(src, yx, dx, dc, to):
        arriving[yx, dx, dc, 0] = push(src, kslot(yx, dx, dc), to)

    def push_v(src, yx, dx, dc, to):
        arriving[yx, dx, dc, 1] = push(src, vslot(yx, dx, dc), to)

    def landed(yx, dx, dc):
        arriving[yx, dx, dc, 0].wait_recv()
        arriving[yx, dx, dc, 1].wait_recv()

    def across(yx, dx):
        push_k(kslot(yx, dx), yx, dx, 1, sibling)
        push_v(vslot(yx, dx), yx, dx, 1, sibling)

    def along_x(yx, k, v):
        push_k(k, yx, 3, 0, at_x(1))
        push_k(k, yx, 1, 0, at_x(-1))
        push_v(v, yx, 3, 0, at_x(1))
        push_v(v, yx, 1, 0, at_x(-1))

    def both(yx, dx):
        landed(yx, dx, 1)

    push_k(tokens(keys, y + toward), 1, 0, 0, at_y(toward))
    push_k(tokens(keys, y - toward), 3, 0, 0, at_y(-toward))
    push_k(tokens(keys, y), 0, 0, 1, sibling)
    push_k(tokens(keys, y), 0, 3, 0, at_x(1))
    push_k(tokens(keys, y), 0, 1, 0, at_x(-1))
    push_v(tokens(values, y + toward), 1, 0, 0, at_y(toward))
    push_v(tokens(values, y - toward), 3, 0, 0, at_y(-toward))
    push_v(tokens(values, y), 0, 0, 1, sibling)
    push_v(tokens(values, y), 0, 3, 0, at_x(1))
    push_v(tokens(values, y), 0, 1, 0, at_x(-1))
    push_k(tokens(keys, y), 0, 2, 0, at_x(2))
    push_v(tokens(values, y), 0, 2, 0, at_x(-2))
    for copy in here:
        copy.wait()

    my_span = (span[row], span[slot_row(1, 0, 0)])

    def hide(side, yx, dx, dc):
        return jnp.where(span[slot_row(yx, dx, dc)] < my_span[side], 0.0, HIDDEN).astype(jnp.float32)

    def at_block(side, block):
        return pl.ds(side * TOK + block * ROWS, ROWS)

    def score(group, side, block):
        query = qbuf[at_block(side, block), :]
        return [
            lax.dot_general(
                query, kbuf[yx, dx].reshape(TOK, HEAD), (((1,), (1,)), ((), ())), preferred_element_type=jnp.float32
            )
            for yx, dx in group
        ]

    def soften(group, side, block, scores, first):
        at = at_block(side, block)
        parts, top = [], None
        for (yx, dx), whole in zip(group, scores):
            for dc in range(2):
                if first and dc == 0 and (yx, side) in ((0, 0), (1, 1)):
                    i = lax.broadcasted_iota(jnp.int32, (ROWS, HEAD), 0) + block * ROWS
                    j = lax.broadcasted_iota(jnp.int32, (ROWS, HEAD), 1) + parity * HALF
                    seen, hidden = i - j, None
                else:
                    seen, hidden = None, hide(side, yx, dx, dc)
                pair = []
                for c in range(2):
                    part = whole[:, dc * HALF + c * HEAD : dc * HALF + (c + 1) * HEAD]
                    if seen is not None:
                        part = jnp.where(seen >= c * HEAD, part, jnp.float32(-HIDDEN))
                    pair.append(part)
                part_top = jnp.maximum(*pair)
                if hidden is not None:
                    part_top = part_top - hidden
                top = part_top if top is None else jnp.maximum(top, part_top)
                parts.append((pair, hidden))
        new = jnp.broadcast_to(jnp.max(top, axis=1, keepdims=True) * SCALE, (ROWS, HEAD))
        keep = None
        if first:
            new = jnp.maximum(new, jnp.float32(FLOOR))
        else:
            old = peak[at, :]
            new = jnp.maximum(old, new)
            keep = jnp.exp2(old - new)
        peak[at, :] = new
        shares = []
        for pair, hidden in parts:
            base = new if hidden is None else new + hidden
            shares += [jnp.exp2(part * SCALE - base).astype(jnp.bfloat16) for part in pair]
        return keep, shares

    def gather_in(group, side, block, keep, shares):
        at = at_block(side, block)
        total = None
        for n, (yx, dx) in enumerate(group):
            share = jnp.concatenate(shares[4 * n : 4 * n + 4], axis=1)
            value = vbuf[yx, dx].reshape(TOK, 2 * HEAD)
            term = jnp.dot(share, value, preferred_element_type=jnp.float32)
            total = term if total is None else total + term
        if keep is None:
            acc[at, :] = total
        else:
            acc[at, :HEAD] = acc[at, :HEAD] * keep + total[:, :HEAD]
            acc[at, HEAD:] = acc[at, HEAD:] * keep + total[:, HEAD:]

    def work(group, sides, first=False, after=None):
        blocks = [(side, block) for side in sides for block in range(NB)]
        scores = score(group, *blocks[0])
        for n, (side, block) in enumerate(blocks):
            later = score(group, *blocks[n + 1]) if n + 1 < len(blocks) else None
            gather_in(group, side, block, *soften(group, side, block, scores, first))
            scores = later
            if after is not None:
                after(side, block)

    half_rows = pl.multiple_of(core * (HEAD // 2), HEAD // 2)
    weights = []

    def send_weights():
        for d in range(1, NZ):
            zz = (z + d) % NZ
            for part, hi in ((0, yhi), (1, 1 - yhi)):
                columns = pl.ds(pl.multiple_of((hi * NZ + zz) * OUT, OUT), OUT)
                weights.append(
                    push(
                        weight.at[pl.ds(half_rows, HEAD // 2), columns],
                        wbuf.at[pl.ds(d * HEAD + half_rows, HEAD // 2), pl.ds(part * OUT, OUT)],
                        at_z(d),
                    )
                )

    def ring_x(yx):
        along_x(yx, kslot(yx, 0), vslot(yx, 0))

    def take(*pairs):
        for yx, dx in pairs:
            landed(yx, dx, 0)
            across(yx, dx)

    def pass_on(yx):
        landed(yx, 3, 0)
        push_k(kslot(yx, 3), yx, 2, 0, at_x(1))
        landed(yx, 1, 0)
        push_v(vslot(yx, 1), yx, 2, 0, at_x(-1))
        across(yx, 3)
        across(yx, 1)

    both(0, 0)
    work(((0, 0),), (0,), True)
    ask = push(queries, qbuf.at[pl.ds(TOK, TOK)], at_y(toward))
    landed(1, 0, 0)
    ring_x(1)
    across(1, 0)
    take((3, 0))
    push_k(tokens(keys, y + 2), 2, 0, 0, at_y(2))
    push_v(tokens(values, y - 2), 2, 0, 0, at_y(-2))
    both(1, 0)
    both(3, 0)
    work(((1, 0), (3, 0)), (0,))
    ring_x(3)
    ask.wait_recv()
    work(((0, 0), (1, 0), (3, 0)), (1,), True)
    send_weights()
    group = ((0, 1), (0, 3), (0, 2))
    take(*group)
    landed(2, 0, 0)
    ring_x(2)
    across(2, 0)
    for pair in group:
        both(*pair)
    work(group, (0, 1))
    pass_on(1)
    group = ((1, 1), (1, 3), (2, 0))
    for pair in group:
        both(*pair)
    work(group, (0, 1))
    pass_on(3)
    group = ((3, 1), (3, 3))
    for pair in group:
        both(*pair)
    work(group, (0, 1))
    pass_on(2)
    take((1, 2))
    group = ((2, 1), (2, 3), (1, 2))
    for pair in group:
        both(*pair)
    work(group, (0, 1))
    for copy in weights:
        copy.wait_recv()
    across_rows = [wbuf.at[pl.ds(d * HEAD + half_rows, HEAD // 2)] for d in range(1, NZ)]
    shared = [push(rows, rows, sibling) for rows in across_rows]
    take((3, 2), (2, 2))
    both(3, 2)
    both(2, 2)

    given = []
    lane = lax.broadcasted_iota(jnp.int32, (STAT, HEAD), 1)

    def hand_over(side, block):
        if side == 0:
            return
        for part in range(block * ROWS // STAT, (block + 1) * ROWS // STAT):
            at, rows = pl.ds(TOK + part * STAT, STAT), pl.ds(part * STAT, STAT)
            give[rows, :] = acc[at, :HEAD].astype(jnp.bfloat16)
            give_stat[part] = jnp.where(lane == 0, peak[at, :], acc[at, HEAD:]).T[:8, :]
            given.append(
                (
                    push(give.at[rows], got.at[rows], at_y(toward)),
                    push(give_stat.at[part], got_stat.at[part], at_y(toward)),
                )
            )

    work(((3, 2), (2, 2)), (1, 0), after=hand_over)

    rings = {}

    def rows_of(cut):
        return pl.ds(cut * CUT, CUT)

    def at_cut(cut, d):
        return around.at[rows_of(cut), pl.ds(d * HEAD, HEAD)]

    def send_z(cut, src, d, hop):
        rings[cut, d] = push(at_cut(cut, src), at_cut(cut, d), at_z(hop))

    def combine(part):
        rows = pl.ds(part * STAT, STAT)
        for copy in given[part]:
            copy.wait_recv()
        stat = jnp.concatenate([got_stat[part], jnp.zeros((STAT - 8, HEAD), jnp.float32)], axis=0).T
        peak_two, sum_two = stat[:, 0:1], stat[:, 1:2]
        peak_one, sum_one = peak[rows, :], acc[rows, HEAD:]
        top = jnp.maximum(peak_one, peak_two)
        one, two = jnp.exp2(peak_one - top), jnp.exp2(peak_two - top)
        total = acc[rows, :HEAD] * one + got[rows, :].astype(jnp.float32) * two
        around[rows, pl.ds(0, HEAD)] = (total / (sum_one * one + sum_two * two)).astype(jnp.bfloat16)

    def begin(cut):
        if cut * CUT % STAT == 0:
            combine(cut * CUT // STAT)
        send_z(cut, 0, 1, 1)
        send_z(cut, 0, NZ - 1, -1)
        if cut in DIRECT:
            send_z(cut, 0, 2, 2)
            send_z(cut, 0, NZ - 2, -2)

    def onward(cut, stage):
        if cut in DIRECT:
            if stage == 1:
                rings[cut, 2].wait_recv()
                send_z(cut, 2, 3, 1)
                if cut % 2 == 0:
                    send_z(cut, 2, 4, 2)
                rings[cut, NZ - 2].wait_recv()
                send_z(cut, NZ - 2, NZ - 3, -1)
                if cut % 2 == 1:
                    send_z(cut, NZ - 2, 4, -2)
            return
        rings[cut, stage].wait_recv()
        if stage < 3 or cut % 2 == 0:
            send_z(cut, stage, stage + 1, 1)
        rings[cut, NZ - stage].wait_recv()
        if stage < 3 or cut % 2 == 1:
            send_z(cut, NZ - stage, NZ - stage - 1, -1)

    swaps = []

    def project(cut):
        for d in (1, 7, 3, 5) if cut in DIRECT else ():
            rings[cut, d].wait_recv()
        rings[cut, 4].wait_recv()
        rows = rows_of(cut)
        part = jnp.dot(around[rows, :], wbuf[...], preferred_element_type=jnp.float32)
        own_part[rows, :] = part[:, :OUT]
        swap[rows, :] = part[:, OUT:].astype(jnp.bfloat16)
        swaps.append(push(swap.at[rows], swapped.at[rows], opposite))

    for copy in shared:
        copy.wait_recv()
    for cut, stage in TURNS:
        if stage == 0:
            begin(cut)
        elif stage == 4:
            project(cut)
        else:
            onward(cut, stage)
    for cut in range(CUTS):
        rows = rows_of(cut)
        swaps[cut].wait_recv()
        out[rows, :] = (own_part[rows, :] + swapped[rows, :].astype(jnp.float32)).astype(jnp.bfloat16)
    for copy in started:
        copy.wait_send()


def local(queries, keys, values, out_weight, slot_span):
    vmem, anywhere = pl.BlockSpec(memory_space=pltpu.VMEM), pl.BlockSpec(memory_space=pl.ANY)
    return pl.pallas_call(
        kernel,
        out_shape=jax.ShapeDtypeStruct((TOK, OUT), jnp.bfloat16),
        in_specs=[pl.BlockSpec(memory_space=pltpu.SMEM), vmem, vmem, vmem, anywhere],
        out_specs=vmem,
        scratch_shapes=[
            pltpu.VMEM((2 * TOK, HEAD), jnp.bfloat16),
            pltpu.VMEM((4, NX, 2, HALF, HEAD), jnp.bfloat16),
            pltpu.VMEM((4, NX, 2, HALF, 2 * HEAD), jnp.bfloat16),
            pltpu.VMEM((NZ * HEAD, 2 * OUT), jnp.bfloat16),
            pltpu.VMEM((2 * TOK, 2 * HEAD), jnp.float32),
            pltpu.VMEM((2 * TOK, HEAD), jnp.float32),
            pltpu.VMEM((TOK, NZ * HEAD), jnp.bfloat16),
            pltpu.VMEM((TOK, HEAD), jnp.bfloat16),
            pltpu.VMEM((TOK, HEAD), jnp.bfloat16),
            pltpu.VMEM((TOK // STAT, 8, STAT), jnp.float32),
            pltpu.VMEM((TOK // STAT, 8, STAT), jnp.float32),
            pltpu.VMEM((TOK, OUT), jnp.float32),
            pltpu.VMEM((TOK, OUT), jnp.bfloat16),
            pltpu.VMEM((TOK, OUT), jnp.bfloat16),
            pltpu.SemaphoreType.DMA((COPIES,)),
            pltpu.SemaphoreType.DMA((COPIES,)),
            pltpu.SemaphoreType.DMA((5,)),
        ],
        compiler_params=pltpu.CompilerParams(
            collective_id=0, has_side_effects=True, vmem_limit_bytes=56 * 2**20
        ),
        cost_estimate=pl.CostEstimate(flops=9 * 10**9, bytes_accessed=3 * 10**6, transcendentals=9 * 10**6),
        name="attend_and_project",
    )(slot_span, queries, keys, values, out_weight)


def solution(mesh):
    in_specs = (P("row", "col"), P("row", None), P("row", None), P("col", None), P())
    return jax.shard_map(local, mesh=mesh, in_specs=in_specs, out_specs=P("row", "col"), check_vma=False)
```

time: 83 us -> 76.3 us (0.919)
  the two profiles are of different devices: /device:TPU:72 before, /device:TPU:17 now
where the time goes in v2:
time: 76.3 us; the launch traced here: 76.1 us
  Pallas kernels  74.4 us (98%)
  local copies, waits for them, and re-layouts  1.67 us (2%)
    pallas_call x1, Pallas kernels, local(): pl.pallas_call(kernel, out_shape=jax.ShapeDtypeStruct((TOK, OUT), jnp.bfl...  74.4 us
    unnamed x1, local copies, waits for them, and re-layouts  1.67 us

profile of v2, /device:TPU:17, one launch (start us, length us, event | category | flops | bytes accessed | tf_op | source)
XLA Modules:
  0.0 76.1 jit_solution(8265088939893664336)
XLA Ops:
  0.0 74.4 %attend_and_project.1 = bf16[512,256]{1,0:T(8,128)(2,1)} custom-call(s32[32]{0:T(128)} %span.1, bf16[512,128]{1,0:T(8,128)(2,1)} %queries.1, bf16[512,512]{1,0:T(8,128)(2,1)} %keys.1, bf16[512,512]{1,0:T(8,128)(2,1)} %values.1, bf16[128,4096]{1,0:T(8,128)(2,1)} %weight.1), custom_call_target="tpu_custom_call" | custom-call | flops 8999999488 | bytes 3000000 | tf_op jit(solution)/shard_map/attend_and_project/pallas_call | solution.py:407
  74.4 1.7 %copy.7 = bf16[512,256]{1,0:T(8,128)(2,1)} copy(bf16[512,256]{1,0:T(8,128)(2,1)} %attend_and_project.1) | data formatting | bytes 524288

commit v3 on v2

--- a/solution.py
+++ b/solution.py
@@ -20,7 +20,6 @@
 HIDDEN = 3e30
 SCALE = HEAD**-0.5 * math.log2(math.e)
 
-LAST = ((2, 2),)
 COPIES = 180
 CUTS = 4
 CUT = TOK // CUTS
@@ -30,8 +29,8 @@
 
 
 def kernel(
-    span, queries, keys, values, weight, out,
-    qbuf, kbuf, vbuf, wbuf, acc, peak, around, give, got, give_stat, got_stat, own_part, swap, swapped,
+    span, queries_in, keys_in, values_in, weight_in, out,
+    queries, keys, values, weight, qbuf, kbuf, vbuf, wbuf, acc, peak, around, give, got, give_stat, got_stat, own_part, swap, swapped,
     send_sem, recv_sem, local_sem,
 ):
     row, col = lax.axis_index("row"), lax.axis_index("col")
@@ -62,10 +61,19 @@
     opposite = device(x, y + 4, z, core)
 
     barrier = pltpu.get_barrier_semaphore()
-    peers = [at_y(toward), at_y(-toward), at_y(2), at_y(-2), opposite, at_x(1), at_x(-1), at_x(2), sibling]
+    peers = [at_y(toward), at_y(-toward), at_y(2), at_y(-2), opposite, at_x(1), at_x(-1), sibling]
     peers += [at_z(d) for d in range(1, NZ)]
     for peer in peers:
         pl.semaphore_signal(barrier, inc=1, device_id=peer, device_id_type=MESH)
+
+    whole = [
+        pltpu.make_async_copy(src, dst, local_sem.at[5 + n])
+        for n, (src, dst) in enumerate(
+            ((keys_in, keys), (values_in, values), (queries_in, queries), (weight_in, weight))
+        )
+    ]
+    for copy in whole:
+        copy.start()
 
     vbuf[:, :, :, :, HEAD:] = jnp.ones((4, NX, 2, HALF, HEAD), jnp.bfloat16)
 
@@ -90,7 +98,12 @@
         pltpu.make_async_copy(weight.at[:, own_weight], wbuf.at[pl.ds(0, HEAD), pl.ds(0, OUT)], local_sem.at[3]),
         pltpu.make_async_copy(weight.at[:, other_weight], wbuf.at[pl.ds(0, HEAD), pl.ds(OUT, OUT)], local_sem.at[4]),
     ]
-    for copy in here:
+    for copy in whole[:3]:
+        copy.wait()
+    for copy in here[:3]:
+        copy.start()
+    whole[3].wait()
+    for copy in here[3:]:
         copy.start()
     pl.semaphore_wait(barrier, len(peers))
 
@@ -140,11 +153,26 @@
     push_v(tokens(values, y), 0, 0, 1, sibling)
     push_v(tokens(values, y), 0, 3, 0, at_x(1))
     push_v(tokens(values, y), 0, 1, 0, at_x(-1))
-    push_k(tokens(keys, y), 0, 2, 0, at_x(2))
-    push_v(tokens(values, y), 0, 2, 0, at_x(-2))
     for copy in here:
         copy.wait()
 
+    half_rows = pl.multiple_of(core * (HEAD // 2), HEAD // 2)
+    weights = []
+
+    def send_weights():
+        for d in range(1, NZ):
+            zz = (z + d) % NZ
+            for part, hi in ((0, yhi), (1, 1 - yhi)):
+                columns = pl.ds(pl.multiple_of((hi * NZ + zz) * OUT, OUT), OUT)
+                weights.append(
+                    push(
+                        weight.at[pl.ds(half_rows, HEAD // 2), columns],
+                        wbuf.at[pl.ds(d * HEAD + half_rows, HEAD // 2), pl.ds(part * OUT, OUT)],
+                        at_z(d),
+                    )
+                )
+
+    send_weights()
     my_span = (span[row], span[slot_row(1, 0, 0)])
 
     def hide(side, yx, dx, dc):
@@ -223,22 +251,6 @@
             if after is not None:
                 after(side, block)
 
-    half_rows = pl.multiple_of(core * (HEAD // 2), HEAD // 2)
-    weights = []
-
-    def send_weights():
-        for d in range(1, NZ):
-            zz = (z + d) % NZ
-            for part, hi in ((0, yhi), (1, 1 - yhi)):
-                columns = pl.ds(pl.multiple_of((hi * NZ + zz) * OUT, OUT), OUT)
-                weights.append(
-                    push(
-                        weight.at[pl.ds(half_rows, HEAD // 2), columns],
-                        wbuf.at[pl.ds(d * HEAD + half_rows, HEAD // 2), pl.ds(part * OUT, OUT)],
-                        at_z(d),
-                    )
-                )
-
     def ring_x(yx):
         along_x(yx, kslot(yx, 0), vslot(yx, 0))
 
@@ -254,6 +266,11 @@
         push_v(vslot(yx, 1), yx, 2, 0, at_x(-1))
         across(yx, 3)
         across(yx, 1)
+
+    def work_on(*group):
+        for pair in group:
+            both(*pair)
+        work(group, (0, 1))
 
     both(0, 0)
     work(((0, 0),), (0,), True)
@@ -264,44 +281,33 @@
     take((3, 0))
     push_k(tokens(keys, y + 2), 2, 0, 0, at_y(2))
     push_v(tokens(values, y - 2), 2, 0, 0, at_y(-2))
+    pass_on(0)
     both(1, 0)
     both(3, 0)
     work(((1, 0), (3, 0)), (0,))
     ring_x(3)
     ask.wait_recv()
     work(((0, 0), (1, 0), (3, 0)), (1,), True)
-    send_weights()
-    group = ((0, 1), (0, 3), (0, 2))
-    take(*group)
     landed(2, 0, 0)
     ring_x(2)
     across(2, 0)
-    for pair in group:
-        both(*pair)
-    work(group, (0, 1))
+    take((0, 2))
+    push_k(kslot(0, 2), 2, 2, 0, at_y(2 - 4 * (ylo // 2)))
+    push_v(vslot(0, 2), 2, 2, 0, at_y(2 - 4 * (ylo // 2)))
+    work_on((0, 1), (0, 3), (2, 0))
     pass_on(1)
-    group = ((1, 1), (1, 3), (2, 0))
-    for pair in group:
-        both(*pair)
-    work(group, (0, 1))
+    work_on((1, 1), (1, 3), (0, 2))
     pass_on(3)
-    group = ((3, 1), (3, 3))
-    for pair in group:
-        both(*pair)
-    work(group, (0, 1))
-    pass_on(2)
-    take((1, 2))
-    group = ((2, 1), (2, 3), (1, 2))
-    for pair in group:
-        both(*pair)
-    work(group, (0, 1))
+    take((2, 2))
+    work_on((3, 1), (3, 3), (2, 2))
+    take((2, 1), (2, 3), (1, 2))
+    work_on((2, 1), (2, 3), (1, 2))
     for copy in weights:
         copy.wait_recv()
     across_rows = [wbuf.at[pl.ds(d * HEAD + half_rows, HEAD // 2)] for d in range(1, NZ)]
     shared = [push(rows, rows, sibling) for rows in across_rows]
-    take((3, 2), (2, 2))
+    take((3, 2))
     both(3, 2)
-    both(2, 2)
 
     given = []
     lane = lax.broadcasted_iota(jnp.int32, (STAT, HEAD), 1)
@@ -320,7 +326,7 @@
                 )
             )
 
-    work(((3, 2), (2, 2)), (1, 0), after=hand_over)
+    work(((3, 2),), (1, 0), after=hand_over)
 
     rings = {}
 
@@ -407,9 +413,13 @@
     return pl.pallas_call(
         kernel,
         out_shape=jax.ShapeDtypeStruct((TOK, OUT), jnp.bfloat16),
-        in_specs=[pl.BlockSpec(memory_space=pltpu.SMEM), vmem, vmem, vmem, anywhere],
+        in_specs=[pl.BlockSpec(memory_space=pltpu.SMEM)] + [anywhere] * 4,
         out_specs=vmem,
         scratch_shapes=[
+            pltpu.VMEM((TOK, HEAD), jnp.bfloat16),
+            pltpu.VMEM((TOK, 4 * HEAD), jnp.bfloat16),
+            pltpu.VMEM((TOK, 4 * HEAD), jnp.bfloat16),
+            pltpu.VMEM((HEAD, 2 * NZ * OUT), jnp.bfloat16),
             pltpu.VMEM((2 * TOK, HEAD), jnp.bfloat16),
             pltpu.VMEM((4, NX, 2, HALF, HEAD), jnp.bfloat16),
             pltpu.VMEM((4, NX, 2, HALF, 2 * HEAD), jnp.bfloat16),
@@ -426,7 +436,7 @@
             pltpu.VMEM((TOK, OUT), jnp.bfloat16),
             pltpu.SemaphoreType.DMA((COPIES,)),
             pltpu.SemaphoreType.DMA((COPIES,)),
-            pltpu.SemaphoreType.DMA((5,)),
+            pltpu.SemaphoreType.DMA((9,)),
         ],
         compiler_params=pltpu.CompilerParams(
             collective_id=0, has_side_effects=True, vmem_limit_bytes=56 * 2**20

time: 76.3 us -> 76.6 us (level)
  the two profiles are of different devices: /device:TPU:17 before, /device:TPU:8 now
where the time goes in v3:
time: 76.6 us; the launch traced here: 76.4 us
  Pallas kernels  74.7 us (98%)
  local copies, waits for them, and re-layouts  1.67 us (2%)
    pallas_call x1, Pallas kernels, local(): pl.pallas_call(kernel, out_shape=jax.ShapeDtypeStruct((TOK, OUT), jnp.bfl...  74.7 us
    unnamed x1, local copies, waits for them, and re-layouts  1.67 us

profile of v3, /device:TPU:8, one launch (start us, length us, event | category | flops | bytes accessed | tf_op | source)
XLA Modules:
  0.0 76.4 jit_solution(2528566460035984896)
XLA Ops:
  0.0 74.7 %attend_and_project.1 = bf16[512,256]{1,0:T(8,128)(2,1)} custom-call(s32[32]{0:T(128)} %span.1, bf16[512,128]{1,0:T(8,128)(2,1)} %queries_in.1, bf16[512,512]{1,0:T(8,128)(2,1)} %keys_in.1, bf16[512,512]{1,0:T(8,128)(2,1)} %values_in.1, bf16[128,4096]{1,0:T(8,128)(2,1)} %weight_in.1), custom_call_target="tpu_custom_call" | custom-call | flops 8999999488 | bytes 3000000 | tf_op jit(solution)/shard_map/attend_and_project/pallas_call | solution.py:413
  74.7 1.7 %copy.7 = bf16[512,256]{1,0:T(8,128)(2,1)} copy(bf16[512,256]{1,0:T(8,128)(2,1)} %attend_and_project.1) | data formatting | bytes 524288

commit v4 on v3

--- a/solution.py
+++ b/solution.py
@@ -267,12 +267,15 @@
         across(yx, 3)
         across(yx, 1)
 
-    def work_on(*group):
+    def ready(*group):
         for pair in group:
             both(*pair)
-        work(group, (0, 1))
-
-    both(0, 0)
+
+    def work_on(*group, between=None):
+        ready(*group)
+        work(group, (0, 1), after=lambda side, block: between() if (side, block) == (0, NB - 1) and between else None)
+
+    ready((0, 0))
     work(((0, 0),), (0,), True)
     ask = push(queries, qbuf.at[pl.ds(TOK, TOK)], at_y(toward))
     landed(1, 0, 0)
@@ -282,8 +285,7 @@
     push_k(tokens(keys, y + 2), 2, 0, 0, at_y(2))
     push_v(tokens(values, y - 2), 2, 0, 0, at_y(-2))
     pass_on(0)
-    both(1, 0)
-    both(3, 0)
+    ready((1, 0), (3, 0))
     work(((1, 0), (3, 0)), (0,))
     ring_x(3)
     ask.wait_recv()
@@ -291,23 +293,28 @@
     landed(2, 0, 0)
     ring_x(2)
     across(2, 0)
-    take((0, 2))
-    push_k(kslot(0, 2), 2, 2, 0, at_y(2 - 4 * (ylo // 2)))
-    push_v(vslot(0, 2), 2, 2, 0, at_y(2 - 4 * (ylo // 2)))
-    work_on((0, 1), (0, 3), (2, 0))
+
+    def far_on():
+        take((0, 2))
+        push_k(kslot(0, 2), 2, 2, 0, at_y(2 - 4 * (ylo // 2)))
+        push_v(vslot(0, 2), 2, 2, 0, at_y(2 - 4 * (ylo // 2)))
+
+    work_on((0, 1), (0, 3), between=far_on)
     pass_on(1)
-    work_on((1, 1), (1, 3), (0, 2))
-    pass_on(3)
+    work_on((2, 0), (0, 2))
+    work_on((1, 1), (1, 3), between=lambda: pass_on(3))
     take((2, 2))
-    work_on((3, 1), (3, 3), (2, 2))
-    take((2, 1), (2, 3), (1, 2))
-    work_on((2, 1), (2, 3), (1, 2))
+    work_on((3, 1), (3, 3), between=lambda: take((2, 1), (2, 3)))
+    take((1, 2))
+    group, last = ((2, 1), (2, 3), (2, 2)), ((1, 2), (3, 2))
+    ready(*group)
+    work(group, (1,))
+    take((3, 2))
     for copy in weights:
         copy.wait_recv()
     across_rows = [wbuf.at[pl.ds(d * HEAD + half_rows, HEAD // 2)] for d in range(1, NZ)]
     shared = [push(rows, rows, sibling) for rows in across_rows]
-    take((3, 2))
-    both(3, 2)
+    ready(*last)
 
     given = []
     lane = lax.broadcasted_iota(jnp.int32, (STAT, HEAD), 1)
@@ -326,7 +333,8 @@
                 )
             )
 
-    work(((3, 2),), (1, 0), after=hand_over)
+    work(last, (1,), after=hand_over)
+    work(group + last, (0,))
 
     rings = {}
 

time: 76.6 us -> 72.7 us (0.949)
  Pallas kernels: 74.7 us -> 70.8 us
    pallas_call x1, Pallas kernels: 74.7 us -> 70.8 us  [local(): pl.pallas_call(kernel, out_shape=jax.ShapeDtypeStruct((TOK, OUT), jnp.bfl...]
where the time goes in v4:
time: 72.7 us; the launch traced here: 72.5 us
  Pallas kernels  70.8 us (97%)
  local copies, waits for them, and re-layouts  1.67 us (2%)
    pallas_call x1, Pallas kernels, local(): pl.pallas_call(kernel, out_shape=jax.ShapeDtypeStruct((TOK, OUT), jnp.bfl...  70.8 us
    unnamed x1, local copies, waits for them, and re-layouts  1.67 us

profile of v4, /device:TPU:8, one launch (start us, length us, event | category | flops | bytes accessed | tf_op | source)
XLA Modules:
  0.0 72.5 jit_solution(1131047737021998039)
XLA Ops:
  0.0 70.8 %attend_and_project.1 = bf16[512,256]{1,0:T(8,128)(2,1)} custom-call(s32[32]{0:T(128)} %span.1, bf16[512,128]{1,0:T(8,128)(2,1)} %queries_in.1, bf16[512,512]{1,0:T(8,128)(2,1)} %keys_in.1, bf16[512,512]{1,0:T(8,128)(2,1)} %values_in.1, bf16[128,4096]{1,0:T(8,128)(2,1)} %weight_in.1), custom_call_target="tpu_custom_call" | custom-call | flops 8999999488 | bytes 3000000 | tf_op jit(solution)/shard_map/attend_and_project/pallas_call | solution.py:421
  70.9 1.7 %copy.7 = bf16[512,256]{1,0:T(8,128)(2,1)} copy(bf16[512,256]{1,0:T(8,128)(2,1)} %attend_and_project.1) | data formatting | bytes 524288

commit v5 on v4

--- a/solution.py
+++ b/solution.py
@@ -25,7 +25,7 @@
 CUT = TOK // CUTS
 LAG = 1
 DIRECT = ()
-TURNS = [(cut, stage) for stage in range(5) for cut in range(CUTS)]
+TURNS = [(0,0),(1,0),(2,0),(3,0),(0,1),(1,1),(2,1),(3,1),(0,2),(1,2),(2,2),(3,2),(0,3),(1,3),(0,4),(2,3),(1,4),(3,3),(2,4),(3,4)]
 
 
 def kernel(
@@ -401,19 +401,30 @@
 
     for copy in shared:
         copy.wait_recv()
+    settled = 0
+
+    def settle(count):
+        nonlocal settled
+        for copy in started[settled:count]:
+            copy.wait_send()
+        settled = max(settled, count)
+
+    before = len(started)
     for cut, stage in TURNS:
+        if (cut, stage) == (0, 1):
+            settle(before)
         if stage == 0:
             begin(cut)
         elif stage == 4:
             project(cut)
         else:
             onward(cut, stage)
+    settle(len(started) - 1)
     for cut in range(CUTS):
         rows = rows_of(cut)
         swaps[cut].wait_recv()
         out[rows, :] = (own_part[rows, :] + swapped[rows, :].astype(jnp.float32)).astype(jnp.bfloat16)
-    for copy in started:
-        copy.wait_send()
+    settle(len(started))
 
 
 def local(queries, keys, values, out_weight, slot_span):

time: 72.7 us -> 72.5 us (level)
  no operation moved by 1% of the time
where the time goes in v5:
time: 72.5 us; the launch traced here: 72.3 us
  Pallas kernels  70.6 us (97%)
  local copies, waits for them, and re-layouts  1.67 us (2%)
    pallas_call x1, Pallas kernels, local(): pl.pallas_call(kernel, out_shape=jax.ShapeDtypeStruct((TOK, OUT), jnp.bfl...  70.6 us
    unnamed x1, local copies, waits for them, and re-layouts  1.67 us

profile of v5, /device:TPU:8, one launch (start us, length us, event | category | flops | bytes accessed | tf_op | source)
XLA Modules:
  0.0 72.3 jit_solution(16359717242815246535)
XLA Ops:
  0.0 70.6 %attend_and_project.1 = bf16[512,256]{1,0:T(8,128)(2,1)} custom-call(s32[32]{0:T(128)} %span.1, bf16[512,128]{1,0:T(8,128)(2,1)} %queries_in.1, bf16[512,512]{1,0:T(8,128)(2,1)} %keys_in.1, bf16[512,512]{1,0:T(8,128)(2,1)} %values_in.1, bf16[128,4096]{1,0:T(8,128)(2,1)} %weight_in.1), custom_call_target="tpu_custom_call" | custom-call | flops 8999999488 | bytes 3000000 | tf_op jit(solution)/shard_map/attend_and_project/pallas_call | solution.py:432
  70.7 1.7 %copy.7 = bf16[512,256]{1,0:T(8,128)(2,1)} copy(bf16[512,256]{1,0:T(8,128)(2,1)} %attend_and_project.1) | data formatting | bytes 524288
